TPU v7x, 256 devices: a whole 4x4x8 slice. The times are simulated.
256 devices in a mesh: rows: 128 (over z, x, y), sub: 2 (over core).
Axes of the slice: x: 4, y: 4, z: 8, core: 2. Of those that a mesh axis runs over, the one named last changes fastest.
Arguments:
- positions: int32 [3, 65536], P(None, ('rows', 'sub')), may hold values from 0 to 19999
- right_side: float32 [32, 65536], P(None, ('rows', 'sub'))
- start_guess: float32 [32, 65536], P(None, ('rows', 'sub')), may hold values from -3 to 3
Outputs:
- solution: float32 [32, 65536], P(None, ('rows', 'sub'))
- residual: float32 [32, 65536], P(None, ('rows', 'sub'))
All inputs are finite; a program needn't handle non-finite values.
Results may differ from a plain program's by a relative error of at most 0.02.
Values may be sent and summed in bfloat16 or wider, within the bound.
A program may use at most 128 MiB of HBM per device.

v0:
```python
import math

import jax
import jax.numpy as jnp
from jax import lax
from jax.sharding import PartitionSpec as P

ITERS = 2


wave_scale = 9.0 / math.pi
ridge = 1.0


def to_metres(positions):
    return positions.astype(jnp.float32) * 0.001


def kernel_tile(column_coords, row_coords):
    squared = jnp.zeros((column_coords.shape[1], row_coords.shape[1]), jnp.float32)
    for component in range(3):
        offsets = column_coords[component][:, None] - row_coords[component][None, :]
        squared = squared + offsets * offsets
    return jnp.sinc(wave_scale * jnp.sqrt(squared)).astype(jnp.bfloat16)


def gram(left, right):
    return jnp.dot(left, right.T, precision=lax.Precision.HIGHEST)


def spd_solve(matrix, targets):
    symmetric = 0.5 * (matrix + matrix.T)
    lower = jnp.linalg.cholesky(symmetric)
    return jax.scipy.linalg.cho_solve((lower, True), targets)


def turned(factor, values_in):
    return jnp.dot(factor.T, values_in, precision=lax.Precision.HIGHEST)


def shards(positions, right_side, start_guess):
    own_coords = to_metres(positions)
    all_coords = lax.all_gather(own_coords, ("rows", "sub"), axis=1, tiled=True)
    total_cols = all_coords.shape[1]
    build_cols = 2048
    build_starts = jnp.arange(total_cols // build_cols, dtype=jnp.int32) * build_cols

    def build_block(first_col):
        columns = lax.dynamic_slice_in_dim(all_coords, first_col, build_cols, 1)
        return kernel_tile(columns, own_coords)

    stored_kernel = lax.map(build_block, build_starts).reshape(total_cols, own_coords.shape[1])

    def kernel_block(first_col, block_cols):
        return lax.dynamic_slice_in_dim(stored_kernel, first_col, block_cols, 0)

    def accumulate(running, segment):
        segment_cols = segment.shape[1]
        block_cols = 2048
        block_count = segment_cols // block_cols

        def add_block(block_index, partial_value):
            offset = block_index * block_cols
            block_dirs = lax.dynamic_slice_in_dim(segment, offset, block_cols, 1)
            return partial_value + jnp.dot(
                block_dirs, kernel_block(offset, block_cols), preferred_element_type=jnp.float32
            )

        return lax.fori_loop(0, block_count, add_block, running)

    def apply_operator(values_in):
        values_bf = values_in.astype(jnp.bfloat16)
        initial = jnp.zeros(values_in.shape, jnp.float32)
        product = accumulate(
            initial, lax.all_gather(values_bf, ("rows", "sub"), axis=1, tiled=True)
        )
        return product + ridge * values_in

    solution = start_guess
    residual = right_side - apply_operator(start_guess)
    direction = residual
    norm_now = lax.psum(gram(residual, residual), ("rows", "sub"))
    for iteration in range(ITERS):
        image = apply_operator(direction)
        curv_sum = lax.psum(gram(direction, image), ("rows", "sub"))
        step_size = spd_solve(curv_sum, norm_now)
        solution = solution + turned(step_size, direction)
        residual = residual - turned(step_size, image)
        if iteration + 1 < ITERS:
            norm_next = lax.psum(gram(residual, residual), ("rows", "sub"))
            correction = spd_solve(norm_now, norm_next)
            direction = residual + turned(correction, direction)
            norm_now = norm_next
    return (solution, residual)


def solution(mesh):
    placed = (P(None, ("rows", "sub")), P(None, ("rows", "sub")), P(None, ("rows", "sub")))
    return jax.shard_map(
        shards,
        mesh=mesh,
        in_specs=placed,
        out_specs=(P(None, ("rows", "sub")), P(None, ("rows", "sub"))),
        check_vma=False,
    )
```

profile of v0, /device:TPU:1, one launch (start us, length us, event | category | flops | bytes accessed | tf_op | source)
XLA Modules:
  0.0 931.9 jit_solution(778442196361430383)
XLA Ops:
  9.4 67.6 %all_gather.13 = f32[3,65536]{1,0:T(4,128)S(1)} all-gather(f32[3,256]{1,0:T(4,128)S(1)} %convert_multiply_fusion), channel_id=1, replica_groups=mesh['rows'=128,'sub'=2] {'rows','sub'}, dimensions={1}, use_global_device_ids=true | all-gather | bytes 789504 | tf_op jit(solution)/shard_map/all_gather | solution.py:43
  76.9 229.8 %while.54 = (s32[]{:T(128)}, bf16[32,2048,256]{2,1,0:T(8,128)(2,1)}, s32[32]{0:T(128)S(1)}, f32[3,65536]{1,0:T(4,128)S(1)}, f32[3,256]{1,0:T(4,128)S(1)}, /*index=5*/s32[]{:T(128)}, s32[]{:T(128)}, s32[]{:T(128)}, s32[]{}, s32[]{}) while((s32[]{:T(128)}, bf16[32,2048,256]{2,1,0:T(8,128)(2,1)}, s32[32]{0:T(128)S(1)}, f32[3,65536]{1,0:T(4,128)S(1)}, ...), condition=%wide.region_1.2_spmd, body=%wide.region_0.1_spmd.sunk | while | flops 22544392 | bytes 1132215 | solution.py:52
  93.9 4.6 fusion.84
  108.3 4.6 fusion.84
  122.7 4.6 fusion.84
  129.8 4.6 fusion.84
  137.0 4.6 fusion.84
  144.2 4.6 fusion.84
  158.6 4.6 fusion.84
  208.8 4.6 fusion.84
  223.2 4.6 fusion.84
  237.5 4.6 fusion.84
  244.7 4.6 fusion.84
  251.9 4.6 fusion.84
  273.5 4.6 fusion.84
  287.8 4.6 fusion.84
  306.7 52.1 %while.55 = (s32[]{:T(128)}, f32[32,256]{1,0:T(8,128)S(1)}, bf16[32,65536]{1,0:T(8,128)(2,1)}, bf16[65536,256]{1,0:T(8,128)(2,1)}, s32[]{:T(128)}, /*index=5*/s32[]{:T(128)}, s32[]{:T(128)}, s32[]{:T(128)}) while((s32[]{:T(128)}, f32[32,256]{1,0:T(8,128)S(1)}, bf16[32,65536]{1,0:T(8,128)(2,1)}, bf16[65536,256]{1,0:T(8,128)(2,1)}, ...), condition=%wide.region_3.4_spmd.clone, body=%wide.region_2.3_spmd.clone.sunk | while | flops 33570824 | bytes 1246860 | solution.py:69
  359.8 104.5 %all-gather.6.cloned.1.call-done = bf16[32,65536]{1,0:T(8,128)(2,1)} async-done(((bf16[32,256]{1,0:T(8,128)(2,1)}), bf16[32,65536]{1,0:T(8,128)(2,1)}) %all-gather.6.cloned.1.call-update) | async-done | bytes 4194320 | tf_op jit(solution)/shard_map/all_gather | solution.py:75
  464.3 52.1 %while.56 = (s32[]{:T(128)}, f32[32,256]{1,0:T(8,128)S(1)}, bf16[32,65536]{1,0:T(8,128)(2,1)}, bf16[65536,256]{1,0:T(8,128)(2,1)}, s32[]{:T(128)}, /*index=5*/s32[]{:T(128)}, s32[]{:T(128)}, s32[]{:T(128)}) while((s32[]{:T(128)}, f32[32,256]{1,0:T(8,128)S(1)}, bf16[32,65536]{1,0:T(8,128)(2,1)}, bf16[65536,256]{1,0:T(8,128)(2,1)}, ...), condition=%wide.region_5.6_spmd.clone, body=%wide.region_4.5_spmd.clone.sunk | while | flops 33570824 | bytes 1246860 | solution.py:69
  516.6 77.2 %all-reduce = (f32[32,32]{1,0:T(8,128)S(1)}, f32[32,32]{1,0:T(8,128)S(1)}) all-reduce(f32[32,32]{1,0:T(8,128)S(1)} %fusion.48, f32[32,32]{1,0:T(8,128)S(1)} %fusion.47), channel_id=1, replica_groups=mesh['rows'=128,'sub'=2] {'rows','sub'}, use_global_device_ids=true, to_apply=%region_9.11 | all-reduce | flops 2048 | bytes 16384 | tf_op jit(solution)/shard_map/psum | solution.py:82
  608.3 72.7 %psum.30 = f32[32,32]{1,0:T(8,128)S(1)} all-reduce(f32[32,32]{1,0:T(8,128)S(1)} %fusion.49), channel_id=1, replica_groups=mesh['rows'=128,'sub'=2] {'rows','sub'}, use_global_device_ids=true, to_apply=%region_10.13 | all-reduce | flops 1024 | bytes 8192 | tf_op jit(solution)/shard_map/psum | solution.py:90
  682.5 104.5 %all-gather.8.cloned.1.call-done = bf16[32,65536]{1,0:T(8,128)(2,1)} async-done(((bf16[32,256]{1,0:T(8,128)(2,1)}), bf16[32,65536]{1,0:T(8,128)(2,1)}) %all-gather.8.cloned.1.call-update) | async-done | bytes 4194320 | tf_op jit(solution)/shard_map/all_gather | solution.py:75
  787.0 52.1 %while.57 = (s32[]{:T(128)}, f32[32,256]{1,0:T(8,128)S(1)}, bf16[32,65536]{1,0:T(8,128)(2,1)}, bf16[65536,256]{1,0:T(8,128)(2,1)}, s32[]{:T(128)}, /*index=5*/s32[]{:T(128)}, s32[]{:T(128)}, s32[]{:T(128)}) while((s32[]{:T(128)}, f32[32,256]{1,0:T(8,128)S(1)}, bf16[32,65536]{1,0:T(8,128)(2,1)}, bf16[65536,256]{1,0:T(8,128)(2,1)}, ...), condition=%wide.region_12.15_spmd.clone, body=%wide.region_11.14_spmd.clone.sunk | while | flops 33570824 | bytes 1246860 | solution.py:69
  839.3 77.1 %psum.31 = f32[32,32]{1,0:T(8,128)S(1)} all-reduce(f32[32,32]{1,0:T(8,128)S(1)} %fusion.50), channel_id=1, replica_groups=mesh['rows'=128,'sub'=2] {'rows','sub'}, use_global_device_ids=true, to_apply=%region_13.16 | all-reduce | flops 1024 | bytes 8192 | tf_op jit(solution)/shard_map/psum | solution.py:85
  (272 shorter events, 286.9 us)
Async XLA Ops:
  7.2 299.6 %all-gather.4.cloned.1.call-start = ((), (), s32[]{:S(2)}) async-start(), calls=%async_computation | async-start | bytes 4210688 | tf_op jit(solution)/shard_map/all_gather | solution.py:75
  8.6 455.7 %all-gather.6.cloned.1.call-start = ((), (), s32[]{:S(2)}) async-start(), calls=%async_computation.1 | async-start | bytes 4210688 | tf_op jit(solution)/shard_map/all_gather | solution.py:75
  306.7 52.2 %copy-start = (f32[32,256]{1,0:T(8,128)S(1)}, f32[32,256]{1,0:T(8,128)}, u32[]{:S(2)}) copy-start(f32[32,256]{1,0:T(8,128)} %param.16) | copy-start | bytes 98308
  306.7 52.2 %copy-start.1 = (f32[32,256]{1,0:T(8,128)S(1)}, f32[32,256]{1,0:T(8,128)}, u32[]{:S(2)}) copy-start(f32[32,256]{1,0:T(8,128)} %param.15) | copy-start | bytes 98308
  359.5 427.4 %all-gather.8.cloned.1.call-start = ((), (), s32[]{:S(2)}) async-start(), calls=%async_computation.2 | async-start | bytes 4210688 | tf_op jit(solution)/shard_map/all_gather | solution.py:75
Sparse Core Ops, SparseCore 0:
  12.3 112.8 all-gather.3
  359.7 104.5 all-gather.5
  682.4 104.5 all-gather.7
where the time goes:
time: 936 us; the launch traced here: 932 us
  blocking collectives  295 us (32%)
  waiting for transfers between devices  209 us (22%)
  other arithmetic  169 us (18%)
  matrix products  158 us (17%)
  loops' own time  63.4 us (7%)
  local copies, waits for them, and re-layouts  23.5 us (3%)
  between operations  14 us (1%)
    all_gather x3, waiting for transfers between devices, apply_operator(): lax.all_gather(values_bf, ('rows', 'sub'), axis=1, tiled=True)  209 us
    dot_general x96, matrix products, add_block(): jnp.dot(block_dirs, kernel_block(offset, block_cols), preferred_element_t...  154 us
    dynamic_update_slice x32, other arithmetic, shards(): lax.map(build_block, build_starts).reshape(total_cols, own_coords.shape[1])  146 us
    psum x1, blocking collectives, shards(): norm_now = lax.psum(gram(residual, residual), ('rows', 'sub'))  77.2 us
    psum x1, blocking collectives, shards(): curv_sum = lax.psum(gram(direction, image), ('rows', 'sub'))  77.1 us
    psum x1, blocking collectives, shards(): norm_next = lax.psum(gram(residual, residual), ('rows', 'sub'))  72.7 us
    all_gather x1, blocking collectives, shards(): all_coords = lax.all_gather(own_coords, ('rows', 'sub'), axis=1, tiled=True)  67.6 us
    another operation x1, loops' own time, shards(): lax.map(build_block, build_starts).reshape(total_cols, own_coords.shape[1])  60.6 us
  transfers between devices with their start and end apart: 3, of which 2 were waited for; matrix products, arithmetic and copies ran while one was open for 18% of the time, Pallas kernels for 0%

commit v1 on v0

v1 whole, which is shorter than its diff:
```python
import jax
import jax.numpy as jnp
from jax import lax
from jax.experimental import pallas as pl
from jax.experimental.pallas import tpu as pltpu
from jax.sharding import PartitionSpec as P

MESH = pl.DeviceIdType.MESH
F32, BF16 = jnp.float32, jnp.bfloat16
HIGHEST = lax.Precision.HIGHEST

RHS = 32
OWN = 256
CHUNK = 2048
HALF = CHUNK // 2
QUARTER = CHUNK // 4
BOTH = 2 * OWN
FEATURES = 16
NZ, NA, NB = 8, 4, 4

SIGMA = (0.009 / (2.0 * 3.141592653589793)) ** 2
SCALE = -1.0 / 0.11181640625
SINE = (-0.1117412088270527, 0.7314446032490506, -1.3877725895638588)
ROUNDER = 12582912.0

ORDER = ((0, 0), (0, 1), (0, 3), (0, 2), (1, 0), (3, 0), (1, 1), (3, 1), (3, 3), (1, 3), (3, 2), (1, 2), (2, 0), (2, 3), (2, 1), (2, 2))
SLOT = {key: place for place, key in enumerate(ORDER)}
CHUNKS = len(ORDER)
GROUPS = (1, 2, 3, 5, 8, 12, 16)

SEMS = {}
for _name in (
    [("z", d) for d in range(1, NZ)]
    + [("b", 1), ("b", 3), ("b", 2, 0), ("b", 2, 1)]
    + [("a", d, db) for d in (1, 2, 3) for db in range(NB)]
    + ["part"]
):
    SEMS[_name] = len(SEMS)
N_SEMS = len(SEMS)
PHASES = (
    [(0, 0, d, 0) for d in range(1, NZ)],
    [(d, 0, 0, s) for d in range(4) for s in range(2) if d + s],
    [(0, d, 0, 0) for d in range(1, 4)],
)
SUM_SEM = {}
for _phase in PHASES:
    for _steps in _phase:
        SUM_SEM[_steps] = len(SUM_SEM)
N_SUM = len(SUM_SEM)


def dot_nt(left, right, precision=None):
    return lax.dot_general(left, right, (((1,), (1,)), ((), ())), precision=precision, preferred_element_type=F32)


def dot_tn(left, right, precision=HIGHEST):
    return lax.dot_general(left, right, (((0,), (0,)), ((), ())), precision=precision, preferred_element_type=F32)


def gram(left, right):
    return dot_nt(left, right, HIGHEST)


def packed(square):
    return jnp.concatenate([square[8 * k : 8 * k + 8] for k in range(4)], axis=1)


def unpacked(rows):
    return jnp.concatenate([rows[:, 32 * k : 32 * k + 32] for k in range(4)], axis=0)


def solve(*systems):
    where = lax.broadcasted_iota(jnp.int32, (RHS, 1), 0)
    work = [jnp.concatenate(pair, axis=1) * (1.0 / jnp.max(pair[0], axis=(0, 1), keepdims=True)) for pair in systems]
    for k in range(0, RHS, 2):
        for index, both in enumerate(work):
            top, low = both[k : k + 1, :], both[k + 1 : k + 2, :]
            a, b = top[:, k : k + 1], top[:, k + 1 : k + 2]
            c, d = low[:, k : k + 1], low[:, k + 1 : k + 2]
            inverse = 1.0 / (a * d - b * c)
            top, low = (d * inverse) * top - (b * inverse) * low, (a * inverse) * low - (c * inverse) * top
            rest = both - both[:, k : k + 1] * top - both[:, k + 1 : k + 2] * low
            work[index] = jnp.where(where == k, top, jnp.where(where == k + 1, low, rest))
    return [both[:, RHS:] for both in work]


def features(positions):
    centred = positions - 10000
    high = (centred + 64) >> 7
    low = centred - high * 128
    norm = jnp.sum(centred * centred, axis=0, keepdims=True)
    rows, factors = [], []
    for k in range(3):
        rows += [high[k : k + 1], low[k : k + 1]]
        own = centred[k : k + 1].astype(F32)
        factors += [own * (-256.0 * SIGMA), own * (-2.0 * SIGMA)]
    for k in range(4):
        rows.append((norm >> (8 * k)) & 255)
        factors.append(jnp.full((1, OWN), SIGMA * 256.0**k, F32))
    rows.append(jnp.ones((1, OWN), jnp.int32))
    factors.append(norm.astype(F32) * SIGMA)
    rows.append(jnp.zeros((FEATURES - len(rows), OWN), jnp.int32))
    factors.append(jnp.zeros((FEATURES - 11, OWN), F32))
    rows = jnp.concatenate(rows, axis=0).astype(F32)
    factors = jnp.concatenate(factors, axis=0)
    first = factors.astype(BF16).astype(F32)
    second = (factors - first).astype(BF16).astype(F32)
    third = factors - first - second
    stack = jnp.concatenate([first, second, third, jnp.zeros((128 - 3 * FEATURES, OWN), F32)], axis=0)
    return rows.astype(BF16), stack.T.astype(BF16)


def begin_values(squared):
    squared = jnp.maximum(squared, 1e-12)
    return squared, lax.rsqrt(squared)


def end_values(squared, inverse):
    turns = squared * inverse
    part = turns - ((turns + ROUNDER) - ROUNDER)
    q = part * part
    value = ((q + SINE[2]) * q + SINE[1]) * q + SINE[0]
    return (value * (part * inverse)).astype(BF16)


def body(
    pos_ref, rhs_ref, start_ref, sol_ref, res_ref,
    kt, v0, v1, v2, lt, phase0, phase1, kept0, kept1, acc, part_out, part_in, r0_ref, q0_ref, p1_ref, sum_a, sum_b,
    send_sems, recv_sems, sum_send, sum_recv, lt_sems,
):
    row, core = lax.axis_index("rows"), lax.axis_index("sub")
    z, rest = row // 16, lax.rem(row, 16)
    x, y = rest // 4, lax.rem(rest, 4)
    a, b = y + core * (x - y), x + core * (y - x)
    step_a, step_b = 1 + 3 * core, 4 - 3 * core

    def device(da=0, db=0, dz=0):
        place = lax.rem(z + dz, NZ) * 16 + lax.rem(a + da, NA) * step_a + lax.rem(b + db, NB) * step_b
        return (place, core)

    def partner(dx, dy, dz, ds):
        place = lax.rem(z + dz, NZ) * 16 + lax.rem(x + dx, 4) * 4 + lax.rem(y + dy, 4)
        return (place, 1 - core if ds else core)

    sibling = (row, 1 - core)

    barrier = pltpu.get_barrier_semaphore()
    greeted = 0
    for steps in SUM_SEM:
        pl.semaphore_signal(barrier, inc=1, device_id=partner(*steps), device_id_type=MESH)
        greeted += 1

    started = []

    def make_gather(number, field):
        def copy(name, src, dst, target):
            return pltpu.make_async_remote_copy(
                src_ref=src, dst_ref=dst,
                send_sem=send_sems.at[number, SEMS[name]], recv_sem=recv_sems.at[number, SEMS[name]],
                device_id=target, device_id_type=MESH,
            )

        def slot(da, db):
            return field.at[SLOT[(da, db)]]

        def z_copy(d):
            src = slot(0, 0)
            return copy(("z", d), src.at[:, 0:OWN], src.at[:, d * OWN : (d + 1) * OWN], device(dz=d))

        def b_copy(d):
            return copy(("b", d), slot(0, 0), slot(0, d), device(db=d))

        def b_half(half):
            cols = slice(half * (CHUNK // 2), (half + 1) * (CHUNK // 2))
            came = 1 if half == 0 else 3
            return copy(("b", 2, half), slot(0, came).at[:, cols], slot(0, 2).at[:, cols], device(db=came))

        def a_copy(d, db):
            if d == 2:
                came = 1 if db in (0, 1) else 3
                return copy(("a", 2, db), slot(came, db), slot(2, db), device(da=came))
            return copy(("a", d, db), slot(0, db), slot(d, db), device(da=d))

        def start(item):
            item.start()
            started.append(item)

        def begin():
            for d in (4, 3, 5, 2, 6, 1, 7):
                start(z_copy(d))

        def arrive(place):
            da, db = ORDER[place]
            if (da, db) == (0, 0):
                for d in range(1, NZ):
                    z_copy(d).wait_recv()
                start(b_copy(1))
                start(b_copy(3))
            elif da == 0:
                if db == 2:
                    b_half(0).wait_recv()
                    b_half(1).wait_recv()
                else:
                    b_copy(db).wait_recv()
                    start(b_half(0 if db == 1 else 1))
            else:
                a_copy(da, db).wait_recv()
                if (da == 1 and db in (0, 1)) or (da == 3 and db in (2, 3)):
                    start(a_copy(2, db))
            if da == 0:
                start(a_copy(1, db))
                start(a_copy(3, db))

        def whole():
            part_out[number] = acc[:, OWN:BOTH]
            item = copy("part", part_out.at[number], part_in.at[number], sibling)
            start(item)
            item.wait_recv()
            return SCALE * (acc[:, 0:OWN] + part_in[number])

        return begin, arrive, whole

    def make_sum(number, buffer):
        def copy(phase_index, steps):
            index = SUM_SEM[steps]
            return pltpu.make_async_remote_copy(
                src_ref=buffer.at[phase_index], dst_ref=buffer.at[3 + index],
                send_sem=sum_send.at[number, index], recv_sem=sum_recv.at[number, index],
                device_id=partner(*steps), device_id_type=MESH,
            )

        def begin(phase_index, value):
            buffer[phase_index] = value
            for steps in PHASES[phase_index]:
                item = copy(phase_index, steps)
                item.start()
                started.append(item)

        def finish(phase_index):
            value = buffer[phase_index]
            for steps in PHASES[phase_index]:
                copy(phase_index, steps).wait_recv()
                value = value + buffer[3 + SUM_SEM[steps]]
            return value

        return begin, finish

    rows, factors = features(pos_ref[...])
    v0[0, 0:RHS, 0:OWN] = start_ref[...].astype(BF16)
    v0[0, RHS : RHS + FEATURES, 0:OWN] = rows
    lt[0:OWN, :] = factors
    acc[...] = jnp.zeros_like(acc)
    kept1[...] = jnp.zeros_like(kept1)
    pl.semaphore_wait(barrier, greeted)

    begin, arrive, whole = make_gather(0, v0)
    begin()
    factors_copy = pltpu.make_async_remote_copy(
        src_ref=lt.at[0:OWN], dst_ref=lt.at[OWN:BOTH], send_sem=lt_sems.at[0], recv_sem=lt_sems.at[1],
        device_id=sibling, device_id_type=MESH,
    )
    factors_copy.start()
    started.append(factors_copy)

    def columns(place, quarter):
        return pl.ds(pl.multiple_of((place % 2) * HALF + quarter * QUARTER, QUARTER), QUARTER)

    def phases(buffer, place, quarter):
        part = v0[place // 2, RHS : RHS + FEATURES, columns(place, quarter)]
        buffer[...] = jnp.dot(
            lt[:, 0 : 3 * FEATURES], jnp.concatenate([part, part, part], axis=0), preferred_element_type=F32
        )

    def values(buffer, kept, place, quarter):
        blocks = [(slice(r, r + 16), slice(c, c + 256)) for c in range(0, QUARTER, 256) for r in range(0, BOTH, 16)]
        ready = begin_values(buffer[blocks[0]])
        for n, block in enumerate(blocks):
            now = ready
            if n + 1 < len(blocks):
                ready = begin_values(buffer[blocks[n + 1]])
            kept[block] = end_values(*now)
        kt[place // 2, :, columns(place, quarter)] = kept[...]

    def apply_quarter(kept, place, quarter):
        acc[...] += dot_nt(v0[place // 2, 0:RHS, columns(place, quarter)], kept[...])

    arrive(0)
    factors_copy.wait_recv()
    come = 1
    for first, last in zip((0,) + GROUPS, GROUPS):
        if first == 0:
            final = 1
        else:
            while come < min(last + 1, CHUNKS):
                arrive(come)
                come += 1
            final = min(2 * last, 2 * CHUNKS - 1)
        if first < 2:
            phases(phase0, 2 * first, 0)

        @pl.loop(2 * first, 2 * last)
        def _(place, final=final):
            phases(phase1, place, 1)
            apply_quarter(kept1, jnp.maximum(place - 1, 0), 1)
            values(phase0, kept0, place, 0)
            phases(phase0, jnp.minimum(place + 1, final), 0)
            apply_quarter(kept0, place, 0)
            values(phase1, kept1, place, 1)

    apply_quarter(kept1, 2 * CHUNKS - 1, 1)

    r0 = rhs_ref[...] - (whole() + start_ref[...])
    r0_ref[...] = r0

    v1[0, :, 0:OWN] = r0.astype(BF16)
    begin, arrive, whole = make_gather(1, v1)
    begin()
    acc[...] = jnp.zeros_like(acc)
    for place in range(CHUNKS):
        arrive(place)
        acc[...] += dot_nt(v1[place], kt[place])
    q0 = whole() + r0_ref[...]
    q0_ref[...] = q0

    v2[0, :, 0:OWN] = q0.astype(BF16)
    begin, arrive, whole = make_gather(2, v2)
    begin()
    sum_begin, sum_finish = make_sum(0, sum_a)
    r0 = r0_ref[...]
    curve = gram(r0, q0)
    curve = 0.5 * (curve + gram(q0, r0))
    sum_begin(0, jnp.concatenate([packed(gram(r0, r0)), packed(curve), packed(gram(q0, q0))], axis=0))
    acc[...] = jnp.zeros_like(acc)
    kept = {}
    for place in range(CHUNKS):
        arrive(place)
        acc[...] += dot_nt(v2[place], kt[place])
        if place in (1, 4):
            index = (1, 4).index(place)
            sum_begin(index + 1, sum_finish(index))
        if place == 11:
            total = sum_finish(2)
            g00, g01, g11 = unpacked(total[0:8]), unpacked(total[8:16]), unpacked(total[16:24])
            identity = (lax.broadcasted_iota(jnp.int32, (RHS, RHS), 0) == lax.broadcasted_iota(jnp.int32, (RHS, RHS), 1)).astype(F32)
            step0, inverse0 = solve((g01, g00), (g00, identity))
            back = jnp.dot(g01, step0, precision=HIGHEST, preferred_element_type=F32)
            bent = jnp.dot(g11, step0, precision=HIGHEST, preferred_element_type=F32)
            norm1 = g00 - back - dot_tn(step0, g01) + dot_tn(step0, bent)
            correction = jnp.dot(inverse0, norm1, precision=HIGHEST, preferred_element_type=F32)
            r0, q0 = r0_ref[...], q0_ref[...]
            r1 = r0 - dot_tn(step0, q0)
            res_ref[...] = r1
            sol_ref[...] = start_ref[...] + dot_tn(step0, r0)
            p1_ref[...] = r1 + dot_tn(correction, r0)
            r0_ref[...] = q0 + dot_tn(correction, q0)
            kept["step0"], kept["norm1"] = step0, norm1
    image = whole() + q0_ref[...]
    q1 = r0_ref[...] - dot_tn(kept["step0"], image)
    p1 = p1_ref[...]
    sum_begin, sum_finish = make_sum(1, sum_b)
    curve = 0.5 * (gram(p1, q1) + gram(q1, p1))
    sum_begin(0, packed(curve))
    for index in range(2):
        sum_begin(index + 1, sum_finish(index))
    (step1,) = solve((unpacked(sum_finish(2)), kept["norm1"]))
    sol_ref[...] += dot_tn(step1, p1)
    res_ref[...] -= dot_tn(step1, q1)

    for item in started:
        item.wait_send()


def shards(positions, right_side, start_guess):
    full = pl.BlockSpec(memory_space=pltpu.VMEM)
    shape = jax.ShapeDtypeStruct((RHS, OWN), F32)
    return pl.pallas_call(
        body,
        out_shape=(shape, shape),
        in_specs=[full] * 3,
        out_specs=(full, full),
        scratch_shapes=[
            pltpu.VMEM((CHUNKS, BOTH, CHUNK), BF16),
            pltpu.VMEM((CHUNKS, RHS + FEATURES, CHUNK), BF16),
            pltpu.VMEM((CHUNKS, RHS, CHUNK), BF16),
            pltpu.VMEM((CHUNKS, RHS, CHUNK), BF16),
            pltpu.VMEM((BOTH, 128), BF16),
            pltpu.VMEM((BOTH, QUARTER), F32),
            pltpu.VMEM((BOTH, QUARTER), F32),
            pltpu.VMEM((BOTH, QUARTER), BF16),
            pltpu.VMEM((BOTH, QUARTER), BF16),
            pltpu.VMEM((RHS, BOTH), F32),
            pltpu.VMEM((3, RHS, OWN), F32),
            pltpu.VMEM((3, RHS, OWN), F32),
            pltpu.VMEM((RHS, OWN), F32),
            pltpu.VMEM((RHS, OWN), F32),
            pltpu.VMEM((RHS, OWN), F32),
            pltpu.VMEM((3 + N_SUM, 24, 128), F32),
            pltpu.VMEM((3 + N_SUM, 8, 128), F32),
            pltpu.SemaphoreType.DMA((3, N_SEMS)),
            pltpu.SemaphoreType.DMA((3, N_SEMS)),
            pltpu.SemaphoreType.DMA((2, N_SUM)),
            pltpu.SemaphoreType.DMA((2, N_SUM)),
            pltpu.SemaphoreType.DMA((2,)),
        ],
        compiler_params=pltpu.CompilerParams(collective_id=0, has_side_effects=True, vmem_limit_bytes=60 * 1024 * 1024),
        name="block_cg",
    )(positions, right_side, start_guess)


def solution(mesh):
    placed = P(None, ("rows", "sub"))
    return jax.shard_map(shards, mesh=mesh, in_specs=(placed,) * 3, out_specs=(placed,) * 2, check_vma=False)
```

time: 936 us -> 148 us (0.16)
  blocking collectives: 295 us -> 0 us
  waiting for transfers between devices: 209 us -> 0 us
  other arithmetic: 169 us -> 0 us
  matrix products: 158 us -> 0 us
  Pallas kernels: 0 us -> 145 us
  loops' own time: 63.4 us -> 0 us
  local copies, waits for them, and re-layouts: 23.5 us -> 2 us
  between operations: 14 us -> 0.65 us
    psum x3 -> x0, blocking collectives: 227 us -> none  [the longest x1 77.2 us: shards(): norm_now = lax.psum(gram(residual, residual), ('rows', 'sub'))]
    all_gather x3 -> x0, waiting for transfers between devices: 209 us -> none  [apply_operator(): lax.all_gather(values_bf, ('rows', 'sub'), axis=1, tiled=True)]
    dot_general x105 -> x0, matrix products: 157 us -> none  [the longest x96 154 us: add_block(): jnp.dot(block_dirs, kernel_block(offset, block_cols), preferred_element_t...]
    dynamic_update_slice x32 -> x0, other arithmetic: 146 us -> none  [shards(): lax.map(build_block, build_starts).reshape(total_cols, own_coords.shape[1])]
    pallas_call x0 -> x1, Pallas kernels: none -> 145 us  [shards(): pl.pallas_call(body, out_shape=(shape, shape), in_specs=[full] * 3, out_s...]
    all_gather x1 -> x0, blocking collectives: 67.6 us -> none  [shards(): all_coords = lax.all_gather(own_coords, ('rows', 'sub'), axis=1, tiled=True)]
    another operation x4 -> x0, loops' own time: 63.4 us -> none  [the longest x1 60.6 us: shards(): lax.map(build_block, build_starts).reshape(total_cols, own_coords.shape[1])]
    another operation x15 -> x0, other arithmetic: 20.1 us -> none  [the longest x9 10.8 us: spd_solve(): lower = jnp.linalg.cholesky(symmetric)]
  transfers between devices with their start and end apart: 3 -> 0, of which waited for: 2 -> 0; matrix products, arithmetic and copies ran while one was open for 18% -> 0% of each run, Pallas kernels for 0% -> 0%
where the time goes in v1:
time: 148 us
  Pallas kernels  145 us (98%)
  local copies, waits for them, and re-layouts  2 us (1%)
    pallas_call x1, Pallas kernels, shards(): pl.pallas_call(body, out_shape=(shape, shape), in_specs=[full] * 3, out_s...  145 us

profile of v1, /device:TPU:1, one launch (start us, length us, event | category | flops | bytes accessed | tf_op | source)
XLA Modules:
  0.0 147.6 jit_solution(6494029124705708810)
XLA Ops:
  0.6 145.0 %block_cg.1 = (f32[32,256]{1,0:T(8,128)}, f32[32,256]{1,0:T(8,128)}) custom-call(s32[3,256]{1,0:T(4,128)} %pos_ref.1, f32[32,256]{1,0:T(8,128)} %rhs_ref.1, f32[32,256]{1,0:T(8,128)} %start_ref.1), custom_call_target="tpu_custom_call" | custom-call | tf_op jit(solution)/shard_map/block_cg/pallas_call | solution.py:376
  145.6 0.0 copy-start
  145.6 1.4 copy.7
  147.0 0.0 copy-done
  147.0 0.6 copy.8
Async XLA Ops:
  145.6 1.4 copy-start

commit v2 on v1

--- a/solution.py
+++ b/solution.py
@@ -69,10 +69,13 @@
     return jnp.concatenate([rows[:, 32 * k : 32 * k + 32] for k in range(4)], axis=0)
 
 
-def solve(*systems):
+def begin_solve(matrix, targets):
+    return jnp.concatenate([matrix, targets], axis=1) * (1.0 / jnp.max(matrix, axis=(0, 1), keepdims=True))
+
+
+def solve_steps(work, first, last):
     where = lax.broadcasted_iota(jnp.int32, (RHS, 1), 0)
-    work = [jnp.concatenate(pair, axis=1) * (1.0 / jnp.max(pair[0], axis=(0, 1), keepdims=True)) for pair in systems]
-    for k in range(0, RHS, 2):
+    for k in range(first, last, 2):
         for index, both in enumerate(work):
             top, low = both[k : k + 1, :], both[k + 1 : k + 2, :]
             a, b = top[:, k : k + 1], top[:, k + 1 : k + 2]
@@ -81,7 +84,10 @@
             top, low = (d * inverse) * top - (b * inverse) * low, (a * inverse) * low - (c * inverse) * top
             rest = both - both[:, k : k + 1] * top - both[:, k + 1 : k + 2] * low
             work[index] = jnp.where(where == k, top, jnp.where(where == k + 1, low, rest))
-    return [both[:, RHS:] for both in work]
+
+
+def dot_nn(left, right):
+    return jnp.dot(left, right, precision=HIGHEST, preferred_element_type=F32)
 
 
 def features(positions):
@@ -125,7 +131,7 @@
 
 def body(
     pos_ref, rhs_ref, start_ref, sol_ref, res_ref,
-    kt, v0, v1, v2, lt, phase0, phase1, kept0, kept1, acc, part_out, part_in, r0_ref, q0_ref, p1_ref, sum_a, sum_b,
+    kt, v0, v1, v2, lt, phase0, phase1, kept0, kept1, acc, part_out, part_in, r0_ref, q0_ref, sum_a, sum_b,
     send_sems, recv_sems, sum_send, sum_recv, lt_sems,
 ):
     row, core = lax.axis_index("rows"), lax.axis_index("sub")
@@ -211,14 +217,18 @@
                 start(a_copy(1, db))
                 start(a_copy(3, db))
 
+        def part():
+            return copy("part", part_out.at[number], part_in.at[number], sibling)
+
+        def share():
+            part_out[number] = acc[:, OWN:BOTH]
+            start(part())
+
         def whole():
-            part_out[number] = acc[:, OWN:BOTH]
-            item = copy("part", part_out.at[number], part_in.at[number], sibling)
-            start(item)
-            item.wait_recv()
+            part().wait_recv()
             return SCALE * (acc[:, 0:OWN] + part_in[number])
 
-        return begin, arrive, whole
+        return begin, arrive, share, whole
 
     def make_sum(number, buffer):
         def copy(phase_index, steps):
@@ -253,7 +263,7 @@
     kept1[...] = jnp.zeros_like(kept1)
     pl.semaphore_wait(barrier, greeted)
 
-    begin, arrive, whole = make_gather(0, v0)
+    begin, arrive, share, whole = make_gather(0, v0)
     begin()
     factors_copy = pltpu.make_async_remote_copy(
         src_ref=lt.at[0:OWN], dst_ref=lt.at[OWN:BOTH], send_sem=lt_sems.at[0], recv_sem=lt_sems.at[1],
@@ -309,60 +319,72 @@
 
     apply_quarter(kept1, 2 * CHUNKS - 1, 1)
 
+    share()
     r0 = rhs_ref[...] - (whole() + start_ref[...])
     r0_ref[...] = r0
 
     v1[0, :, 0:OWN] = r0.astype(BF16)
-    begin, arrive, whole = make_gather(1, v1)
+    begin, arrive, share, whole = make_gather(1, v1)
     begin()
     acc[...] = jnp.zeros_like(acc)
     for place in range(CHUNKS):
         arrive(place)
         acc[...] += dot_nt(v1[place], kt[place])
+    share()
     q0 = whole() + r0_ref[...]
-    q0_ref[...] = q0
+    q0_ref[:, 0:OWN] = q0
 
     v2[0, :, 0:OWN] = q0.astype(BF16)
-    begin, arrive, whole = make_gather(2, v2)
+    begin, arrive, share, whole = make_gather(2, v2)
     begin()
     sum_begin, sum_finish = make_sum(0, sum_a)
     r0 = r0_ref[...]
     curve = gram(r0, q0)
     curve = 0.5 * (curve + gram(q0, r0))
     sum_begin(0, jnp.concatenate([packed(gram(r0, r0)), packed(curve), packed(gram(q0, q0))], axis=0))
+    q0_copy = pltpu.make_async_remote_copy(
+        src_ref=q0_ref.at[:, 0:OWN], dst_ref=q0_ref.at[:, OWN:BOTH], send_sem=lt_sems.at[2], recv_sem=lt_sems.at[3],
+        device_id=sibling, device_id_type=MESH,
+    )
+    q0_copy.start()
+    started.append(q0_copy)
     acc[...] = jnp.zeros_like(acc)
-    kept = {}
     for place in range(CHUNKS):
         arrive(place)
         acc[...] += dot_nt(v2[place], kt[place])
         if place in (1, 4):
             index = (1, 4).index(place)
             sum_begin(index + 1, sum_finish(index))
-        if place == 11:
-            total = sum_finish(2)
-            g00, g01, g11 = unpacked(total[0:8]), unpacked(total[8:16]), unpacked(total[16:24])
-            identity = (lax.broadcasted_iota(jnp.int32, (RHS, RHS), 0) == lax.broadcasted_iota(jnp.int32, (RHS, RHS), 1)).astype(F32)
-            step0, inverse0 = solve((g01, g00), (g00, identity))
-            back = jnp.dot(g01, step0, precision=HIGHEST, preferred_element_type=F32)
-            bent = jnp.dot(g11, step0, precision=HIGHEST, preferred_element_type=F32)
-            norm1 = g00 - back - dot_tn(step0, g01) + dot_tn(step0, bent)
-            correction = jnp.dot(inverse0, norm1, precision=HIGHEST, preferred_element_type=F32)
-            r0, q0 = r0_ref[...], q0_ref[...]
-            r1 = r0 - dot_tn(step0, q0)
-            res_ref[...] = r1
-            sol_ref[...] = start_ref[...] + dot_tn(step0, r0)
-            p1_ref[...] = r1 + dot_tn(correction, r0)
-            r0_ref[...] = q0 + dot_tn(correction, q0)
-            kept["step0"], kept["norm1"] = step0, norm1
-    image = whole() + q0_ref[...]
-    q1 = r0_ref[...] - dot_tn(kept["step0"], image)
-    p1 = p1_ref[...]
-    sum_begin, sum_finish = make_sum(1, sum_b)
-    curve = 0.5 * (gram(p1, q1) + gram(q1, p1))
-    sum_begin(0, packed(curve))
-    for index in range(2):
-        sum_begin(index + 1, sum_finish(index))
-    (step1,) = solve((unpacked(sum_finish(2)), kept["norm1"]))
+    q0_copy.wait_recv()
+
+    chip_q0, product = q0_ref[...], acc[...]
+    last_begin, last_finish = make_sum(1, sum_b)
+    last_begin(0, packed((0.5 * SCALE) * (gram(chip_q0, product) + gram(product, chip_q0))))
+    share()
+    total = sum_finish(2)
+    g00, g01, g11 = unpacked(total[0:8]), unpacked(total[8:16]), unpacked(total[16:24])
+    identity = (lax.broadcasted_iota(jnp.int32, (RHS, RHS), 0) == lax.broadcasted_iota(jnp.int32, (RHS, RHS), 1)).astype(F32)
+    work = [begin_solve(g01, g00), begin_solve(g00, identity)]
+    solve_steps(work, 0, RHS // 2)
+    last_begin(1, last_finish(0))
+    solve_steps(work, RHS // 2, RHS)
+    step0, inverse0 = work[0][:, RHS:], work[1][:, RHS:]
+    back, bent = dot_nn(g01, step0), dot_nn(g11, step0)
+    norm1 = g00 - back - dot_tn(step0, g01) + dot_tn(step0, bent)
+    last_begin(2, last_finish(1))
+    keep = identity + dot_nn(inverse0, norm1)
+    cross = dot_tn(bent, keep)
+    fixed = dot_tn(keep, dot_nn(g01, keep) - bent) - cross + dot_tn(step0, bent)
+    r0, q0 = r0_ref[...], q0_ref[:, 0:OWN]
+    image = whole() + q0
+    turned = dot_tn(step0, q0)
+    p1 = dot_tn(keep, r0) - turned
+    q1 = dot_tn(keep, q0) - dot_tn(step0, image)
+    sol_ref[...] = start_ref[...] + dot_tn(step0, r0)
+    res_ref[...] = r0 - turned
+    work = [begin_solve(fixed + dot_tn(step0, dot_nn(unpacked(last_finish(2)), step0)), norm1)]
+    solve_steps(work, 0, RHS)
+    step1 = work[0][:, RHS:]
     sol_ref[...] += dot_tn(step1, p1)
     res_ref[...] -= dot_tn(step1, q1)
 
@@ -392,15 +414,14 @@
             pltpu.VMEM((3, RHS, OWN), F32),
             pltpu.VMEM((3, RHS, OWN), F32),
             pltpu.VMEM((RHS, OWN), F32),
-            pltpu.VMEM((RHS, OWN), F32),
-            pltpu.VMEM((RHS, OWN), F32),
+            pltpu.VMEM((RHS, BOTH), F32),
             pltpu.VMEM((3 + N_SUM, 24, 128), F32),
             pltpu.VMEM((3 + N_SUM, 8, 128), F32),
             pltpu.SemaphoreType.DMA((3, N_SEMS)),
             pltpu.SemaphoreType.DMA((3, N_SEMS)),
             pltpu.SemaphoreType.DMA((2, N_SUM)),
             pltpu.SemaphoreType.DMA((2, N_SUM)),
-            pltpu.SemaphoreType.DMA((2,)),
+            pltpu.SemaphoreType.DMA((4,)),
         ],
         compiler_params=pltpu.CompilerParams(collective_id=0, has_side_effects=True, vmem_limit_bytes=60 * 1024 * 1024),
         name="block_cg",

time: 148 us -> 146 us (0.986)
  Pallas kernels: 145 us -> 143 us
    pallas_call x1, Pallas kernels: 145 us -> 143 us  [shards(): pl.pallas_call(body, out_shape=(shape, shape), in_specs=[full] * 3, out_s...]
where the time goes in v2:
time: 146 us
  Pallas kernels  143 us (98%)
  local copies, waits for them, and re-layouts  2 us (1%)
    pallas_call x1, Pallas kernels, shards(): pl.pallas_call(body, out_shape=(shape, shape), in_specs=[full] * 3, out_s...  143 us

profile of v2, /device:TPU:1, one launch (start us, length us, event | category | flops | bytes accessed | tf_op | source)
XLA Modules:
  0.0 145.8 jit_solution(1864979690744943631)
XLA Ops:
  0.6 143.2 %block_cg.1 = (f32[32,256]{1,0:T(8,128)}, f32[32,256]{1,0:T(8,128)}) custom-call(s32[3,256]{1,0:T(4,128)} %pos_ref.1, f32[32,256]{1,0:T(8,128)} %rhs_ref.1, f32[32,256]{1,0:T(8,128)} %start_ref.1), custom_call_target="tpu_custom_call" | custom-call | tf_op jit(solution)/shard_map/block_cg/pallas_call | solution.py:398
  143.8 0.0 copy-start
  143.8 1.4 copy.7
  145.2 0.0 copy-done
  145.2 0.6 copy.8
Async XLA Ops:
  143.8 1.4 copy-start

commit v3 on v2

--- a/solution.py
+++ b/solution.py
@@ -1,3 +1,5 @@
+import functools
+
 import jax
 import jax.numpy as jnp
 from jax import lax
@@ -26,7 +28,6 @@
 ORDER = ((0, 0), (0, 1), (0, 3), (0, 2), (1, 0), (3, 0), (1, 1), (3, 1), (3, 3), (1, 3), (3, 2), (1, 2), (2, 0), (2, 3), (2, 1), (2, 2))
 SLOT = {key: place for place, key in enumerate(ORDER)}
 CHUNKS = len(ORDER)
-GROUPS = (1, 2, 3, 5, 8, 12, 16)
 
 SEMS = {}
 for _name in (
@@ -187,42 +188,42 @@
                 return copy(("a", 2, db), slot(came, db), slot(2, db), device(da=came))
             return copy(("a", d, db), slot(0, db), slot(d, db), device(da=d))
 
-        def start(item):
-            item.start()
-            started.append(item)
+        def start(make, *which):
+            make(*which).start()
+            started.append(functools.partial(make, *which))
 
         def begin():
             for d in (4, 3, 5, 2, 6, 1, 7):
-                start(z_copy(d))
+                start(z_copy, d)
 
         def arrive(place):
             da, db = ORDER[place]
             if (da, db) == (0, 0):
                 for d in range(1, NZ):
                     z_copy(d).wait_recv()
-                start(b_copy(1))
-                start(b_copy(3))
+                start(b_copy, 1)
+                start(b_copy, 3)
             elif da == 0:
                 if db == 2:
                     b_half(0).wait_recv()
                     b_half(1).wait_recv()
                 else:
                     b_copy(db).wait_recv()
-                    start(b_half(0 if db == 1 else 1))
+                    start(b_half, 0 if db == 1 else 1)
             else:
                 a_copy(da, db).wait_recv()
                 if (da == 1 and db in (0, 1)) or (da == 3 and db in (2, 3)):
-                    start(a_copy(2, db))
+                    start(a_copy, 2, db)
             if da == 0:
-                start(a_copy(1, db))
-                start(a_copy(3, db))
+                start(a_copy, 1, db)
+                start(a_copy, 3, db)
 
         def part():
             return copy("part", part_out.at[number], part_in.at[number], sibling)
 
         def share():
             part_out[number] = acc[:, OWN:BOTH]
-            start(part())
+            start(part)
 
         def whole():
             part().wait_recv()
@@ -242,9 +243,8 @@
         def begin(phase_index, value):
             buffer[phase_index] = value
             for steps in PHASES[phase_index]:
-                item = copy(phase_index, steps)
-                item.start()
-                started.append(item)
+                copy(phase_index, steps).start()
+                started.append(functools.partial(copy, phase_index, steps))
 
         def finish(phase_index):
             value = buffer[phase_index]
@@ -265,11 +265,12 @@
 
     begin, arrive, share, whole = make_gather(0, v0)
     begin()
-    factors_copy = pltpu.make_async_remote_copy(
+    factors_copy = functools.partial(
+        pltpu.make_async_remote_copy,
         src_ref=lt.at[0:OWN], dst_ref=lt.at[OWN:BOTH], send_sem=lt_sems.at[0], recv_sem=lt_sems.at[1],
         device_id=sibling, device_id_type=MESH,
     )
-    factors_copy.start()
+    factors_copy().start()
     started.append(factors_copy)
 
     def columns(place, quarter):
@@ -294,26 +295,33 @@
     def apply_quarter(kept, place, quarter):
         acc[...] += dot_nt(v0[place // 2, 0:RHS, columns(place, quarter)], kept[...])
 
+    def at(chunk, function, which):
+        for place in which:
+            pl.when(chunk == place)(functools.partial(function, place))
+
+    def look_ahead(place):
+        if place == 1:
+            arrive(1)
+        if place + 1 < CHUNKS:
+            arrive(place + 1)
+        if place == 1:
+            phases(phase0, 2, 0)
+
     arrive(0)
-    factors_copy.wait_recv()
-    come = 1
-    for first, last in zip((0,) + GROUPS, GROUPS):
-        if first == 0:
-            final = 1
-        else:
-            while come < min(last + 1, CHUNKS):
-                arrive(come)
-                come += 1
-            final = min(2 * last, 2 * CHUNKS - 1)
-        if first < 2:
-            phases(phase0, 2 * first, 0)
-
-        @pl.loop(2 * first, 2 * last)
-        def _(place, final=final):
+    factors_copy().wait_recv()
+    phases(phase0, 0, 0)
+
+    @pl.loop(0, CHUNKS)
+    def _(chunk):
+        at(chunk, look_ahead, range(1, CHUNKS - 1))
+
+        @pl.loop(2 * chunk, 2 * chunk + 2)
+        def _(place):
+            later = jnp.where(jnp.logical_or(place == 1, place == 2 * CHUNKS - 1), place, place + 1)
             phases(phase1, place, 1)
             apply_quarter(kept1, jnp.maximum(place - 1, 0), 1)
             values(phase0, kept0, place, 0)
-            phases(phase0, jnp.minimum(place + 1, final), 0)
+            phases(phase0, later, 0)
             apply_quarter(kept0, place, 0)
             values(phase1, kept1, place, 1)
 
@@ -327,9 +335,12 @@
     begin, arrive, share, whole = make_gather(1, v1)
     begin()
     acc[...] = jnp.zeros_like(acc)
-    for place in range(CHUNKS):
-        arrive(place)
-        acc[...] += dot_nt(v1[place], kt[place])
+
+    @pl.loop(0, CHUNKS)
+    def _(chunk):
+        at(chunk, arrive, range(CHUNKS))
+        acc[...] += dot_nt(v1[chunk], kt[chunk])
+
     share()
     q0 = whole() + r0_ref[...]
     q0_ref[:, 0:OWN] = q0
@@ -342,20 +353,27 @@
     curve = gram(r0, q0)
     curve = 0.5 * (curve + gram(q0, r0))
     sum_begin(0, jnp.concatenate([packed(gram(r0, r0)), packed(curve), packed(gram(q0, q0))], axis=0))
-    q0_copy = pltpu.make_async_remote_copy(
+    q0_copy = functools.partial(
+        pltpu.make_async_remote_copy,
         src_ref=q0_ref.at[:, 0:OWN], dst_ref=q0_ref.at[:, OWN:BOTH], send_sem=lt_sems.at[2], recv_sem=lt_sems.at[3],
         device_id=sibling, device_id_type=MESH,
     )
-    q0_copy.start()
+    q0_copy().start()
     started.append(q0_copy)
     acc[...] = jnp.zeros_like(acc)
-    for place in range(CHUNKS):
+
+    def arrive_and_sum(place):
+        if place in (2, 5):
+            index = (2, 5).index(place)
+            sum_begin(index + 1, sum_finish(index))
         arrive(place)
-        acc[...] += dot_nt(v2[place], kt[place])
-        if place in (1, 4):
-            index = (1, 4).index(place)
-            sum_begin(index + 1, sum_finish(index))
-    q0_copy.wait_recv()
+
+    @pl.loop(0, CHUNKS)
+    def _(chunk):
+        at(chunk, arrive_and_sum, range(CHUNKS))
+        acc[...] += dot_nt(v2[chunk], kt[chunk])
+
+    q0_copy().wait_recv()
 
     chip_q0, product = q0_ref[...], acc[...]
     last_begin, last_finish = make_sum(1, sum_b)
@@ -388,8 +406,8 @@
     sol_ref[...] += dot_tn(step1, p1)
     res_ref[...] -= dot_tn(step1, q1)
 
-    for item in started:
-        item.wait_send()
+    for make in started:
+        make().wait_send()
 
 
 def shards(positions, right_side, start_guess):

time: 146 us -> 148 us (1.014)
  Pallas kernels: 143 us -> 145 us
    pallas_call x1, Pallas kernels: 143 us -> 145 us  [shards(): pl.pallas_call(body, out_shape=(shape, shape), in_specs=[full] * 3, out_s...]
where the time goes in v3:
time: 148 us
  Pallas kernels  145 us (98%)
  local copies, waits for them, and re-layouts  2 us (1%)
    pallas_call x1, Pallas kernels, shards(): pl.pallas_call(body, out_shape=(shape, shape), in_specs=[full] * 3, out_s...  145 us

profile of v3, /device:TPU:1, one launch (start us, length us, event | category | flops | bytes accessed | tf_op | source)
XLA Modules:
  0.0 147.8 jit_solution(11430943482013867374)
XLA Ops:
  0.6 145.1 %block_cg.1 = (f32[32,256]{1,0:T(8,128)}, f32[32,256]{1,0:T(8,128)}) custom-call(s32[3,256]{1,0:T(4,128)} %pos_ref.1, f32[32,256]{1,0:T(8,128)} %rhs_ref.1, f32[32,256]{1,0:T(8,128)} %start_ref.1), custom_call_target="tpu_custom_call" | custom-call | tf_op jit(solution)/shard_map/block_cg/pallas_call | solution.py:416
  145.8 0.0 copy-start
  145.8 1.4 copy.7
  147.2 0.0 copy-done
  147.2 0.6 copy.8
Async XLA Ops:
  145.8 1.4 copy-start

commit v4 on v3

--- a/solution.py
+++ b/solution.py
@@ -23,9 +23,9 @@
 SIGMA = (0.009 / (2.0 * 3.141592653589793)) ** 2
 SCALE = -1.0 / 0.11181640625
 SINE = (-0.1117412088270527, 0.7314446032490506, -1.3877725895638588)
-ROUNDER = 12582912.0
 
 ORDER = ((0, 0), (0, 1), (0, 3), (0, 2), (1, 0), (3, 0), (1, 1), (3, 1), (3, 3), (1, 3), (3, 2), (1, 2), (2, 0), (2, 3), (2, 1), (2, 2))
+LOOK = (0, 2, 3, 4, 6, 7, 8, 10, 11, 11, 11, 11, 12, 13, 14, 15)
 SLOT = {key: place for place, key in enumerate(ORDER)}
 CHUNKS = len(ORDER)
 
@@ -124,7 +124,7 @@
 
 def end_values(squared, inverse):
     turns = squared * inverse
-    part = turns - ((turns + ROUNDER) - ROUNDER)
+    part = turns - jnp.round(turns)
     q = part * part
     value = ((q + SINE[2]) * q + SINE[1]) * q + SINE[0]
     return (value * (part * inverse)).astype(BF16)
@@ -331,6 +331,10 @@
     r0 = rhs_ref[...] - (whole() + start_ref[...])
     r0_ref[...] = r0
 
+    def arrivals(place):
+        for come in range(LOOK[place - 1] + 1 if place else 0, LOOK[place] + 1):
+            arrive(come)
+
     v1[0, :, 0:OWN] = r0.astype(BF16)
     begin, arrive, share, whole = make_gather(1, v1)
     begin()
@@ -338,7 +342,7 @@
 
     @pl.loop(0, CHUNKS)
     def _(chunk):
-        at(chunk, arrive, range(CHUNKS))
+        at(chunk, arrivals, range(CHUNKS))
         acc[...] += dot_nt(v1[chunk], kt[chunk])
 
     share()
@@ -366,7 +370,7 @@
         if place in (2, 5):
             index = (2, 5).index(place)
             sum_begin(index + 1, sum_finish(index))
-        arrive(place)
+        arrivals(place)
 
     @pl.loop(0, CHUNKS)
     def _(chunk):

time: 148 us -> 149 us (level)
  no operation moved by 1% of the time
where the time goes in v4:
time: 149 us; the launch traced here: 148 us
  Pallas kernels  146 us (98%)
  local copies, waits for them, and re-layouts  2 us (1%)
    pallas_call x1, Pallas kernels, shards(): pl.pallas_call(body, out_shape=(shape, shape), in_specs=[full] * 3, out_s...  146 us

profile of v4, /device:TPU:1, one launch (start us, length us, event | category | flops | bytes accessed | tf_op | source)
XLA Modules:
  0.0 148.5 jit_solution(13387427817582097406)
XLA Ops:
  0.6 145.8 %block_cg.1 = (f32[32,256]{1,0:T(8,128)}, f32[32,256]{1,0:T(8,128)}) custom-call(s32[3,256]{1,0:T(4,128)} %pos_ref.1, f32[32,256]{1,0:T(8,128)} %rhs_ref.1, f32[32,256]{1,0:T(8,128)} %start_ref.1), custom_call_target="tpu_custom_call" | custom-call | tf_op jit(solution)/shard_map/block_cg/pallas_call | solution.py:420
  146.5 0.0 copy-start
  146.5 1.4 copy.7
  147.9 0.0 copy-done
  147.9 0.6 copy.8
Async XLA Ops:
  146.5 1.4 copy-start

commit v5 on v3

--- a/solution.py
+++ b/solution.py
@@ -132,7 +132,7 @@
 
 def body(
     pos_ref, rhs_ref, start_ref, sol_ref, res_ref,
-    kt, v0, v1, v2, lt, phase0, phase1, kept0, kept1, acc, part_out, part_in, r0_ref, q0_ref, sum_a, sum_b,
+    kt, v0, v1, v2, lt, phase0, phase1, kept0, kept1, acc, acc_t, part_out, part_in, r0_ref, q0_ref, sum_a, sum_b,
     send_sems, recv_sems, sum_send, sum_recv, lt_sems,
 ):
     row, core = lax.axis_index("rows"), lax.axis_index("sub")
@@ -331,16 +331,24 @@
     r0 = rhs_ref[...] - (whole() + start_ref[...])
     r0_ref[...] = r0
 
+    def apply_chunk(field, chunk):
+        own_part = dot_nt(field[chunk], kt[chunk, 0:OWN])
+        other_part = dot_nt(kt[chunk, OWN:BOTH], field[chunk])
+        acc[:, 0:OWN] += own_part
+        acc_t[...] += other_part
+
     v1[0, :, 0:OWN] = r0.astype(BF16)
     begin, arrive, share, whole = make_gather(1, v1)
     begin()
     acc[...] = jnp.zeros_like(acc)
+    acc_t[...] = jnp.zeros_like(acc_t)
 
     @pl.loop(0, CHUNKS)
     def _(chunk):
         at(chunk, arrive, range(CHUNKS))
-        acc[...] += dot_nt(v1[chunk], kt[chunk])
-
+        apply_chunk(v1, chunk)
+
+    acc[:, OWN:BOTH] = acc_t[...].T
     share()
     q0 = whole() + r0_ref[...]
     q0_ref[:, 0:OWN] = q0
@@ -361,6 +369,7 @@
     q0_copy().start()
     started.append(q0_copy)
     acc[...] = jnp.zeros_like(acc)
+    acc_t[...] = jnp.zeros_like(acc_t)
 
     def arrive_and_sum(place):
         if place in (2, 5):
@@ -371,9 +380,10 @@
     @pl.loop(0, CHUNKS)
     def _(chunk):
         at(chunk, arrive_and_sum, range(CHUNKS))
-        acc[...] += dot_nt(v2[chunk], kt[chunk])
+        apply_chunk(v2, chunk)
 
     q0_copy().wait_recv()
+    acc[:, OWN:BOTH] = acc_t[...].T
 
     chip_q0, product = q0_ref[...], acc[...]
     last_begin, last_finish = make_sum(1, sum_b)
@@ -429,6 +439,7 @@
             pltpu.VMEM((BOTH, QUARTER), BF16),
             pltpu.VMEM((BOTH, QUARTER), BF16),
             pltpu.VMEM((RHS, BOTH), F32),
+            pltpu.VMEM((OWN, RHS), F32),
             pltpu.VMEM((3, RHS, OWN), F32),
             pltpu.VMEM((3, RHS, OWN), F32),
             pltpu.VMEM((RHS, OWN), F32),

time: 148 us -> 149 us (level)
  no operation moved by 1% of the time
where the time goes in v5:
time: 149 us; the launch traced here: 148 us
  Pallas kernels  146 us (98%)
  local copies, waits for them, and re-layouts  2 us (1%)
    pallas_call x1, Pallas kernels, shards(): pl.pallas_call(body, out_shape=(shape, shape), in_specs=[full] * 3, out_s...  146 us

profile of v5, /device:TPU:1, one launch (start us, length us, event | category | flops | bytes accessed | tf_op | source)
XLA Modules:
  0.0 148.3 jit_solution(8558375707363952741)
XLA Ops:
  0.6 145.7 %block_cg.1 = (f32[32,256]{1,0:T(8,128)}, f32[32,256]{1,0:T(8,128)}) custom-call(s32[3,256]{1,0:T(4,128)} %pos_ref.1, f32[32,256]{1,0:T(8,128)} %rhs_ref.1, f32[32,256]{1,0:T(8,128)} %start_ref.1), custom_call_target="tpu_custom_call" | custom-call | tf_op jit(solution)/shard_map/block_cg/pallas_call | solution.py:426
  146.3 0.0 copy-start
  146.3 1.4 copy.7
  147.7 0.0 copy-done
  147.7 0.6 copy.8
Async XLA Ops:
  146.3 1.4 copy-start

commit v6 on v2

--- a/solution.py
+++ b/solution.py
@@ -278,7 +278,7 @@
     def phases(buffer, place, quarter):
         part = v0[place // 2, RHS : RHS + FEATURES, columns(place, quarter)]
         buffer[...] = jnp.dot(
-            lt[:, 0 : 3 * FEATURES], jnp.concatenate([part, part, part], axis=0), preferred_element_type=F32
+            lt[...], jnp.concatenate([part] * (128 // FEATURES), axis=0), preferred_element_type=F32
         )
 
     def values(buffer, kept, place, quarter):

time: 146 us -> 148 us (1.014)
  Pallas kernels: 143 us -> 145 us
    pallas_call x1, Pallas kernels: 143 us -> 145 us  [shards(): pl.pallas_call(body, out_shape=(shape, shape), in_specs=[full] * 3, out_s...]
where the time goes in v6:
time: 148 us; the launch traced here: 147 us
  Pallas kernels  145 us (98%)
  local copies, waits for them, and re-layouts  2 us (1%)
    pallas_call x1, Pallas kernels, shards(): pl.pallas_call(body, out_shape=(shape, shape), in_specs=[full] * 3, out_s...  145 us

profile of v6, /device:TPU:1, one launch (start us, length us, event | category | flops | bytes accessed | tf_op | source)
XLA Modules:
  0.0 147.5 jit_solution(2719547450458203262)
XLA Ops:
  0.6 144.8 %block_cg.1 = (f32[32,256]{1,0:T(8,128)}, f32[32,256]{1,0:T(8,128)}) custom-call(s32[3,256]{1,0:T(4,128)} %pos_ref.1, f32[32,256]{1,0:T(8,128)} %rhs_ref.1, f32[32,256]{1,0:T(8,128)} %start_ref.1), custom_call_target="tpu_custom_call" | custom-call | tf_op jit(solution)/shard_map/block_cg/pallas_call | solution.py:398
  145.4 0.0 copy-start
  145.5 1.4 copy.7
  146.8 0.0 copy-done
  146.8 0.6 copy.8
Async XLA Ops:
  145.4 1.4 copy-start

commit v7 on v4

--- a/solution.py
+++ b/solution.py
@@ -20,6 +20,7 @@
 FEATURES = 16
 NZ, NA, NB = 8, 4, 4
 
+ROUNDER = 12582912.0
 SIGMA = (0.009 / (2.0 * 3.141592653589793)) ** 2
 SCALE = -1.0 / 0.11181640625
 SINE = (-0.1117412088270527, 0.7314446032490506, -1.3877725895638588)
@@ -124,7 +125,7 @@
 
 def end_values(squared, inverse):
     turns = squared * inverse
-    part = turns - jnp.round(turns)
+    part = turns - ((turns + ROUNDER) - ROUNDER)
     q = part * part
     value = ((q + SINE[2]) * q + SINE[1]) * q + SINE[0]
     return (value * (part * inverse)).astype(BF16)

time: 149 us -> 148 us (level)
  no operation moved by 1% of the time
where the time goes in v7:
time: 148 us
  Pallas kernels  146 us (99%)
  local copies, waits for them, and re-layouts  2 us (1%)
    pallas_call x1, Pallas kernels, shards(): pl.pallas_call(body, out_shape=(shape, shape), in_specs=[full] * 3, out_s...  146 us

profile of v7, /device:TPU:1, one launch (start us, length us, event | category | flops | bytes accessed | tf_op | source)
XLA Modules:
  0.0 148.2 jit_solution(17037200434619882306)
XLA Ops:
  0.6 145.6 %block_cg.1 = (f32[32,256]{1,0:T(8,128)}, f32[32,256]{1,0:T(8,128)}) custom-call(s32[3,256]{1,0:T(4,128)} %pos_ref.1, f32[32,256]{1,0:T(8,128)} %rhs_ref.1, f32[32,256]{1,0:T(8,128)} %start_ref.1), custom_call_target="tpu_custom_call" | custom-call | tf_op jit(solution)/shard_map/block_cg/pallas_call | solution.py:421
  146.2 0.0 copy-start
  146.2 1.4 copy.7
  147.6 0.0 copy-done
  147.6 0.6 copy.8
Async XLA Ops:
  146.2 1.4 copy-start
